TPU v7x, 256 devices: a whole 4x4x8 slice. The times are simulated.
256 devices in a mesh: section: 8 (over y_hi, x), dp: 32 (over y_lo, z, core).
Axes of the slice: x: 4, y: 4 (y_hi: 2, y_lo: 2; y = y_hi * 2 + y_lo), z: 8, core: 2. Of those that a mesh axis runs over, the one named last changes fastest.
Arguments:
- section_inputs: bfloat16 [8, 4096, 2048], P('section', 'dp'), as said below
- section_weights: bfloat16 [8, 2048, 2048], P('section'), may hold values from -0.125 to 0.125
- memory_weights: bfloat16 [8, 2048, 2048], P('section', 'dp'), may hold values from -0.125 to 0.125
- norm_gains: float32 [8, 2048], P('section'), may hold values from 0.1 to 1.9
- memory: bfloat16 [4096, 2048], P('dp'), may hold values from -5 to 5
- cotangent: bfloat16 [4096, 2048], P('dp'), may hold values from -3 to 3
- lengths: int32 [32], P('dp'), may hold values from 32 to 128, as said below
Outputs:
- input_grads: bfloat16 [8, 4096, 2048], P('section', 'dp')
- weight_grads: float32 [8, 2048, 2048], P('section', 'dp')
- gain_grads: float32 [8, 2048], P('section', 'dp')
Inputs may be any that keep to these rules, and one draw needn't show every extreme that they name: `section_inputs`: saved activations with uneven scales over tokens and features. `lengths`: tokens of a sequence at positions below its entry are live, the rest padding; some sequence is full and some has 32 live tokens.
All inputs are finite; a program needn't handle non-finite values.
Results may differ from a plain program's by a relative error of at most 0.035.
Values may be sent and summed in bfloat16 or wider, within the bound.
A program may use at most 128 MiB of HBM per device.

v0:
```python
import functools

import jax
import jax.numpy as jnp
from jax import lax
from jax.experimental import pallas as pl
from jax.experimental.pallas import tpu as pltpu
from jax.sharding import PartitionSpec as P

epsilon = 1e-06
BF = jnp.bfloat16
F32 = jnp.float32
CH = 16
TILE = 256


def arrived(ref, sem, dev):
    pltpu.make_async_remote_copy(
        src_ref=ref, dst_ref=ref, send_sem=sem, recv_sem=sem, device_id=dev,
        device_id_type=pl.DeviceIdType.MESH).wait_recv()


def left(ref, sem, dev):
    pltpu.make_async_remote_copy(
        src_ref=ref, dst_ref=ref, send_sem=sem, recv_sem=sem, device_id=dev,
        device_id_type=pl.DeviceIdType.MESH).wait_send()


class Gather:
    def __init__(self, buf, rows, place, send_sem, recv_sems, lane=None):
        self.buf, self.rows, self.place = buf, rows, place
        self.y, self.z, self.c, self.nz, self.device = place
        self.lane = self.c if lane is None else lane
        self.far = self.nz // 2
        self.ss, self.rs = send_sem, recv_sems
        self.mate = self.device(self.y, self.z, 1 - self.c)

    @staticmethod
    def count(nz):
        return 5 * (nz // 2) + 3

    def block(self, q, start, size):
        return self.buf.at[pl.ds(pl.multiple_of((q * 2 + self.lane) * self.rows + start, 16), size)]

    def copy(self, q, start, size, ident, dev):
        ref = self.block(q, start, size)
        return pltpu.make_async_remote_copy(
            src_ref=ref, dst_ref=ref, send_sem=self.ss.at[0], recv_sem=self.rs.at[ident],
            device_id=dev, device_id_type=pl.DeviceIdType.MESH)

    def await_rows(self, rows, ident):
        arrived(self.buf.at[pl.ds(0, rows)], self.rs.at[ident], self.mate)

    def turn(self, z):
        return lax.rem(z + 2 * self.nz, self.nz)

    def source(self, way, d):
        return self.turn(self.z - (1 - 2 * way) * d)

    def ways(self, d, m=0):
        return (0,) if d == 0 or (d == self.far and m == 1) else (0, 1)

    def span(self, way, d, m):
        half, quarter = self.rows // 2, self.rows // 4
        if m in (1, 3):
            return (half if m == 1 else half + quarter), quarter
        return (way * quarter, quarter) if d == self.far else (0, half)

    def z_copy(self, way, d, m):
        y = 1 - self.y if m == 2 else self.y
        start, size = self.span(way, d, m)
        dev = self.device(self.y, self.turn(self.z + 1 - 2 * way), self.c)
        return self.copy(y * self.nz + self.source(way, d - 1), start, size, 3 * (d - 1) + m, dev)

    def y_copy(self, way, d):
        start, size = self.span(way, d, 1)
        dev = self.device(1 - self.y, self.z, self.c)
        return self.copy(self.y * self.nz + self.source(way, d), start, size, 3 * self.far + d, dev)

    def first_copy(self):
        dev = self.device(1 - self.y, self.z, self.c)
        return self.copy(self.y * self.nz + self.z, 0, self.rows // 2, 4 * self.far + 1, dev)

    def hand(self, kind, args):
        ident = 4 * self.far + 2
        if kind in ("own", "first"):
            y = self.y if kind == "own" else 1 - self.y
            self.copy(y * self.nz + self.z, 0, self.size(kind, args), ident, self.mate).start()
            return
        way, d, m = args
        start, size = self.span(way, d, 3 if kind == "back" else m)
        y = {"z": 1 - self.y if m == 2 else self.y, "back": 1 - self.y if m else self.y, "y": 1 - self.y}[kind]
        self.copy(y * self.nz + self.source(way, d), start, size, ident + d, self.mate).start()

    def size(self, kind, args):
        if kind in ("own", "first"):
            return self.rows if kind == "own" else self.rows // 2
        way, d, m = args
        return self.span(way, d, 3 if kind == "back" else m)[1]

    def begin(self):
        self.first_copy().start()
        for m in (1, 0):
            for way in (0, 1):
                self.z_copy(way, 1, m).start()
        self.y_copy(0, 0).start()
        self.hand("own", ())

    def begin_other(self):
        self.await_rows(self.rows // 2, 4 * self.far + 1)
        for way in (0, 1):
            self.z_copy(way, 1, 2).start()
        self.hand("first", ())

    def pair_step(self, i):
        d, m = i // 3 + 1, (1, 0, 2)[i % 3]
        self.await_rows(sum(self.span(way, d, m)[1] for way in self.ways(d, m)), 3 * (d - 1) + m)
        if d < self.far:
            for way in self.ways(d + 1, m):
                self.z_copy(way, d + 1, m).start()
        for way in self.ways(d, m):
            if m == 1:
                self.y_copy(way, d).start()
            self.hand("z", (way, d, m))

    def backs(self, d):
        if d == 0:
            return [(0, 0, 1)]
        return [(0, d, 0), (1, d, 1)] if d == self.far else [(way, d, m) for m in (0, 1) for way in (0, 1)]

    def crossed(self, d):
        return [(way, d, 1) for way in self.ways(d, 1)]

    def handed(self, d):
        if d == 0:
            came = [("own", ()), ("first", ())]
        else:
            came = [("z", (way, d, m)) for m in (0, 1, 2) for way in self.ways(d, m)]
        return came + [("back", args) for args in self.backs(d)] + [("y", args) for args in self.crossed(d)]

    def pass_backs(self, d, relay):
        relay.await_back(d)
        for args in self.backs(d):
            self.hand("back", args)
        self.await_rows(sum(self.size("y", args) for args in self.crossed(d)), 3 * self.far + d)
        for args in self.crossed(d):
            self.hand("y", args)

    def collect(self, d):
        self.await_rows(sum(self.size(*h) for h in self.handed(d)), 4 * self.far + 2 + d)

    def sent(self):
        total = self.rows // 2
        for d in range(self.far + 1):
            total += sum(self.size("y", args) for args in self.crossed(d))
            total += sum(self.size(*h) * (2 if h[0] == "z" else 1) for h in self.handed(d))
        left(self.buf.at[pl.ds(0, total)], self.ss.at[0], self.mate)

    def sources(self, d):
        spots = {0: (0,), self.far: (self.far,)}.get(d, (d, -d))
        return [y * self.nz + self.turn(self.z + o) for o in spots for y in (0, 1)]


class Relay:
    def __init__(self, gather, section, half, sems):
        self.g, self.ss, self.rs = gather, *sems
        g = gather
        self.quarter = g.rows // 4
        self.partner = {
            "section": jnp.where(section >= half, section - half, section + half),
            "dp": ((1 - g.y) * g.nz + g.z) * 2 + g.c,
        }

    @staticmethod
    def count(nz):
        return 3 + 3 * (nz // 2)

    def copy(self, y, src, ident, dev):
        g = self.g
        start, size = g.span(0, 1, 3)
        ref = g.block(y * g.nz + src, start, size)
        return pltpu.make_async_remote_copy(
            src_ref=ref, dst_ref=ref, send_sem=self.ss.at[0], recv_sem=self.rs.at[ident],
            device_id=dev, device_id_type=pl.DeviceIdType.MESH)

    def await_quarters(self, number, ident):
        arrived(self.g.buf.at[pl.ds(0, number * self.quarter)], self.rs.at[ident], self.partner)

    def await_back(self, d):
        self.await_quarters(len(self.g.backs(d)), 2 + 2 * self.g.far + d)

    def up(self):
        return self.copy(self.g.y, self.g.z, 0, self.partner)

    def ring(self, way, d, m):
        g = self.g
        dev = g.device(g.y, g.turn(g.z + 1 - 2 * way), g.c)
        return self.copy(g.y if m else 1 - g.y, g.source(way, d - 1), 2 + 2 * (d - 1) + m, dev)

    def back(self, way, d, m):
        g = self.g
        return self.copy(g.y if m else 1 - g.y, g.source(way, d), 2 + 2 * g.far + d, self.partner)

    def begin(self):
        g = self.g
        self.await_quarters(1, 0)
        self.copy(1 - g.y, g.z, 1, g.device(1 - g.y, g.z, g.c)).start()
        for way in (0, 1):
            self.ring(way, 1, 0).start()

    def begin_other(self):
        self.await_quarters(1, 1)
        for way in (0, 1):
            self.ring(way, 1, 1).start()
        self.back(0, 0, 1).start()

    def step(self, d):
        g = self.g
        for m in (0, 1):
            came = [args for args in g.backs(d) if args[2] == m]
            self.await_quarters(len(came), 2 + 2 * (d - 1) + m)
            for way, _, _ in came:
                if d < g.far and (way, d + 1, m) in g.backs(d + 1):
                    self.ring(way, d + 1, m).start()
                self.back(way, d, m).start()

    def sent(self, encoder):
        number = 2 + 2 * sum(len(self.g.backs(d)) for d in range(1, self.g.far + 1)) if encoder else 1
        left(self.g.buf.at[pl.ds(0, number * self.quarter)], self.ss.at[0], self.partner)


class HalfGather:
    def __init__(self, buf, place, send_sem, recv_sems):
        self.buf, self.ss, self.rs = buf, send_sem, recv_sems
        self.y, self.z, self.c, self.nz, self.device = place
        self.far = self.nz // 2
        self.rows = buf.shape[1]
        self.mate = self.device(self.y, self.z, 1 - self.c)

    @staticmethod
    def count(nz):
        return 1 + 2 * (nz // 2)

    def turn(self, z):
        return lax.rem(z + 2 * self.nz, self.nz)

    def cross(self, src):
        return pltpu.make_async_remote_copy(
            src_ref=src, dst_ref=self.buf.at[self.y * self.nz + self.z], send_sem=self.ss.at[0],
            recv_sem=self.rs.at[0], device_id=self.device(1 - self.y, self.z, self.c),
            device_id_type=pl.DeviceIdType.MESH)

    def z_copy(self, way, d, m):
        sign = 1 - 2 * way
        src = self.turn(self.z - sign * (d - 1))
        y = 1 - self.y if m else self.y
        size = self.rows // 2 if d == self.far else self.rows
        ref = self.buf.at[y * self.nz + src, pl.ds(way * size if d == self.far else 0, size)]
        return pltpu.make_async_remote_copy(
            src_ref=ref, dst_ref=ref, send_sem=self.ss.at[0], recv_sem=self.rs.at[1 + 2 * (d - 1) + m],
            device_id=self.device(self.y, self.turn(self.z + sign), self.c), device_id_type=pl.DeviceIdType.MESH)

    def begin(self):
        for way in (0, 1):
            self.z_copy(way, 1, 0).start()

    def begin_other(self):
        arrived(self.buf.at[0], self.rs.at[0], self.mate)
        for way in (0, 1):
            self.z_copy(way, 1, 1).start()

    def pair_step(self, i):
        d, m = i // 2 + 1, i % 2
        arrived(self.buf.at[pl.ds(0, 1 if d == self.far else 2)], self.rs.at[1 + i], self.mate)
        if d < self.far:
            for way in (0, 1):
                self.z_copy(way, d + 1, m).start()

    def sent(self):
        left(self.buf.at[pl.ds(0, 2 * self.nz - 1)], self.ss.at[0], self.mate)


def relay_kernel(n_sec, n_dp,
                 x_hbm, w_hbm, mw_hbm, gain_ref, mem_hbm, cot_hbm, len_ref,
                 gin_hbm, og, gg_ref,
                 x_ref, mem_ref, cot_ref, gin_ref,
                 wv, wt, mwv, mwt, sc, sg, normed, slope, act, gate, dwt, inv, gbuf, tbuf, tsend,
                 gpv, gacc, gs, ts, gpg, gpt, dws, dwp, dwo, gnv, gng, gnl, gnp,
                 load_sem, wag_s, wag_r, rel_s, rel_r, sag_s, sag_r, g_s, g_r, t_s, t_r, late_s, late_r, pass_s, pass_r, swap_s, swap_r,
                 tail_s, tail_r):
    s = lax.axis_index("section")
    j = lax.axis_index("dp")
    half = n_sec // 2
    nq = n_dp // 2
    nz = nq // 2
    c = lax.rem(j, 2)
    q0 = j // 2
    y, z = q0 // nz, lax.rem(q0, nz)
    toks, feats = x_ref.shape
    rw = mw_hbm.shape[0]
    n_ch = toks // CH
    tiles = feats // TILE
    decoder = s >= half
    encoder = s < half
    above = n_sec - 1 - s
    MESH = pl.DeviceIdType.MESH

    def device(yy, zz, cc):
        return {"dp": (yy * nz + zz) * 2 + cc}

    def load(src, dst, i):
        copy = pltpu.make_async_copy(src, dst, load_sem.at[i])
        copy.start()
        return copy

    barrier = pltpu.get_barrier_semaphore()

    def greet(i, carry):
        q = lax.rem(q0 + i, nq)
        pl.semaphore_signal(barrier, inc=1, device_id={"dp": q * 2 + c}, device_id_type=MESH)
        return carry

    lax.fori_loop(1, nq, greet, 0)
    pl.semaphore_signal(barrier, inc=1, device_id={"dp": q0 * 2 + 1 - c}, device_id_type=MESH)

    @pl.when(s > 0)
    def _():
        pl.semaphore_signal(barrier, inc=1, device_id={"section": s - 1}, device_id_type=MESH)

    @pl.when(s < n_sec - 1)
    def _():
        pl.semaphore_signal(barrier, inc=1, device_id={"section": s + 1}, device_id_type=MESH)

    load_m = pltpu.make_async_copy(
        mw_hbm, mwv.at[pl.ds(pl.multiple_of(j * rw, rw), rw)], load_sem.at[1])

    @pl.when(decoder)
    def _():
        load_m.start()

    load_x = load(x_hbm, x_ref, 2)
    load_w = load(w_hbm, wv, 0)
    load_mem = load(mem_hbm, mem_ref, 3)
    load_cot = load(cot_hbm, cot_ref, 4)

    pl.semaphore_signal(
        barrier, inc=1, device_id={"section": lax.rem(s + half, n_sec), "dp": ((1 - y) * nz + z) * 2 + c},
        device_id_type=MESH)
    ends = (s == 0) | (s == n_sec - 1)
    pl.semaphore_wait(barrier, nq + jnp.where(ends, 2, 3))

    place = (y, z, c, nz, device)

    wag = Gather(mwv, rw, place, wag_s, wag_r)
    relay = Relay(wag, s, half, (rel_s, rel_r))
    sag = HalfGather(sg, place, sag_s, sag_r)
    far = wag.far
    last_pair = 2 * far
    width = feats // 2
    cols_z = feats // nz
    mine, theirs = (pl.ds(pl.multiple_of(v * width, width), width) for v in (y, 1 - y))
    crossing = sc.at[:, theirs]
    mine_z = pl.ds(pl.multiple_of(z * cols_z, cols_z), cols_z)

    @pl.when(decoder)
    def _():
        load_m.wait()
        relay.up().start()
        wag.begin()

    def rows_of(k):
        return pl.ds(pl.multiple_of(k * CH, CH), CH)

    def norm_rows(k, carry):
        rows = rows_of(k)
        wide = x_ref[rows, :].astype(F32)
        scale = lax.rsqrt(jnp.mean(wide * wide, axis=1, keepdims=True) + epsilon)
        inv[rows, :] = jnp.broadcast_to(scale, (CH, 128))
        value = wide * scale
        normed[rows, :] = value
        sc[rows, :] = (value * gain_ref[...]).astype(BF)
        sg[q0, rows, :] = sc[rows, mine]
        return carry

    load_x.wait()
    lax.fori_loop(0, n_ch, norm_rows, 0)

    @pl.when(encoder)
    def _():
        sag.cross(crossing).start()
        relay.begin()

    load_w.wait()

    def cols_of(t):
        return pl.ds(pl.multiple_of(t * TILE, TILE), TILE)

    def preact_tile(t, carry):
        cols = cols_of(t)
        p = jnp.dot(sc[...], wv[:, cols], preferred_element_type=F32)
        sig = jax.nn.sigmoid(p)
        act[:, cols] = p * sig
        slope[:, cols] = sig * (1.0 + p * (1.0 - sig))
        return carry

    lax.fori_loop(0, tiles // 2, preact_tile, 0)

    @pl.when(encoder)
    def _():
        relay.begin_other()
        relay.step(1)

    lax.fori_loop(tiles // 2, tiles, preact_tile, 0)
    load_mem.wait()
    load_cot.wait()

    def turn_w(piece, pieces):
        def body(i, carry):
            a, b = i // tiles, lax.rem(i, tiles)
            wt[cols_of(b), cols_of(a)] = wv[cols_of(a), cols_of(b)].T
            return carry

        size = tiles * tiles // pieces
        lax.fori_loop(piece * size, (piece + 1) * size, body, 0, unroll=4)

    def chip_rows(q):
        return pl.ds(pl.multiple_of(q * 2 * rw, 2 * rw), 2 * rw)

    def turn_m(d):
        spots = [chip_rows(q) for q in wag.sources(d)]

        def body(t, carry):
            for at in spots:
                mwt[cols_of(t), at] = mwv[at, cols_of(t)].T
            return carry

        lax.fori_loop(0, tiles, body, 0, unroll=2)

    def gate_part(d):
        spots = [chip_rows(q) for q in wag.sources(d)]
        left = jnp.concatenate([mem_ref[:, at] for at in spots], axis=1)

        def body(t, carry):
            cols = cols_of(t)
            right = jnp.concatenate([mwv[at, cols] for at in spots], axis=0)
            p = jnp.dot(left, right, preferred_element_type=F32)
            if d == 0:
                gate[:, cols] = p
            elif d < far:
                gate[:, cols] += p
            else:
                slope[:, cols] = slope[:, cols] * (gate[:, cols] + p)
            return carry

        lax.fori_loop(0, tiles, body, 0, unroll=4)

    @pl.when(decoder)
    def _():
        wag.begin_other()
        wag.pair_step(0)
        turn_w(0, 4)
        wag.pair_step(1)
        turn_w(1, 4)
        wag.pair_step(2)
        turn_w(2, 4)
        wag.pair_step(3)
        turn_w(3, 4)
        wag.pair_step(4)
        wag.pass_backs(0, relay)
        wag.pair_step(5)
        sag.cross(crossing).start()
        wag.collect(0)
        gate_part(0)
        turn_m(0)
        wag.pair_step(6)
        wag.pass_backs(1, relay)
        wag.pair_step(7)
        wag.collect(1)
        gate_part(1)
        wag.pair_step(8)
        turn_m(1)
        wag.pass_backs(2, relay)
        wag.pair_step(9)
        wag.collect(2)
        gate_part(2)
        wag.pair_step(10)
        turn_m(2)
        wag.pair_step(11)
        wag.pass_backs(3, relay)
        wag.pass_backs(4, relay)
        wag.collect(3)
        gate_part(3)
        turn_m(3)
        wag.collect(4)
        gate_part(4)
        sag.begin()
        turn_m(4)

        @pl.when(above >= 2)
        def _():
            sag.begin_other()
            sag.pair_step(0)

        @pl.when(above >= 3)
        def _():
            sag.pair_step(1)

    @pl.when(encoder)
    def _():
        relay.step(2)
        turn_w(0, 4)
        relay.step(3)
        turn_w(1, 4)
        relay.step(4)
        sag.begin()
        sag.begin_other()
        turn_w(2, 4)
        turn_w(3, 4)
        for i in range(last_pair - 2):
            sag.pair_step(i)

    @pl.when(s == n_sec - 1)
    def _():
        live = lax.broadcasted_iota(jnp.int32, (toks, TILE), 0) < len_ref[0]

        def body(t, carry):
            cols = cols_of(t)
            gbuf[:, cols] = jnp.where(live, cot_ref[:, cols], jnp.zeros((), BF))
            return carry

        lax.fori_loop(0, tiles, body, 0)

    gacc[...] = jnp.zeros_like(gacc)

    def down(src, dst, k, send_sems, recv_sems):
        rows = rows_of(k)
        return pltpu.make_async_remote_copy(
            src_ref=src.at[rows], dst_ref=dst.at[rows], send_sem=send_sems.at[0], recv_sem=recv_sems.at[k],
            device_id={"section": s - 1}, device_id_type=MESH)

    groups = [(0, 3 * CH), (3 * CH, 2 * CH), (5 * CH, CH), (6 * CH, CH), (7 * CH, CH)]
    direct = (2, 3, 4)
    round_z = [nz // 2] + [v for i in range(nz // 2 - 1, 0, -1) for v in (i, nz - i)]

    def late_send(g):
        start, size = groups[g]
        rows = pl.ds(start, size)

        def send(yy, zz):
            pltpu.make_async_remote_copy(
                src_ref=gpv.at[rows, pl.ds(pl.multiple_of(zz * cols_z, cols_z), cols_z)], dst_ref=gpg.at[q0, rows],
                send_sem=late_s.at[0], recv_sem=late_r.at[g], device_id=device(yy, zz, c), device_id_type=MESH).start()

        for i in round_z:
            send(y, lax.rem(z + i, nz))
        if g in direct:
            @pl.when(encoder)
            def _():
                for i in round_z + [0]:
                    send(1 - y, lax.rem(z + i, nz))

    def late_done(g, count):
        start, size = groups[g]
        ref = gpg.at[pl.ds(0, count), pl.ds(start, size)]
        return pltpu.make_async_remote_copy(
            src_ref=ref, dst_ref=ref, send_sem=late_s.at[0], recv_sem=late_r.at[g],
            device_id={"dp": q0 * 2 + 1 - c}, device_id_type=MESH)

    def late_recv(g):
        if g not in direct:
            late_done(g, nz - 1).wait_recv()
            return

        @pl.when(encoder)
        def _():
            late_done(g, nq - 1).wait_recv()

        @pl.when(decoder)
        def _():
            late_done(g, nz - 1).wait_recv()

    def late_pass(g):
        start, size = groups[g]
        ref = gpg.at[pl.ds(pl.multiple_of(y * nz, nz), nz), pl.ds(start, size)]
        return pltpu.make_async_remote_copy(
            src_ref=ref, dst_ref=ref, send_sem=pass_s.at[0], recv_sem=pass_r.at[g],
            device_id=device(1 - y, z, c), device_id_type=MESH)

    def term(k):
        rows = rows_of(k)
        up = gbuf[rows, :].astype(F32)
        grad_gate = (up * act[rows, :]).astype(BF)
        for t in range(tiles):
            cols = slice(t * TILE, (t + 1) * TILE)
            ts[:, cols] = jnp.dot(grad_gate, mwt[:, cols], preferred_element_type=F32)

        @pl.when(s < n_sec - 1)
        def _():
            down(tsend, tbuf, k, t_s, t_r).wait_recv()
            tsend[rows, :] = (ts[...] + tbuf[rows, :].astype(F32)).astype(BF)

        @pl.when(s == n_sec - 1)
        def _():
            tsend[rows, :] = ts[...].astype(BF)

    passing = [(0, 3, 0), (0, 7, 1), (1, 1, 0), (1, 3, 1), (1, 6, 2), (2, 1, 1), (2, 4, 2), (2, 6, 3),
               (3, 1, 2), (3, 4, 3), (3, 6, 4)]

    def own_rows(g):
        rows = pl.ds(groups[g][0], groups[g][1])
        gpg[q0, rows, :] = gpv[rows, mine_z]

    def chunk(k, carry):
        rows = rows_of(k)

        @pl.when(s < n_sec - 1)
        def _():
            down(gin_ref, gbuf, k, g_s, g_r).wait_recv()

        @pl.when(s == half)
        def _():
            term(k)
            down(tsend, gbuf, k, t_s, g_r).start()

        gpv[rows, :] = (gbuf[rows, :].astype(F32) * slope[rows, :]).astype(BF)
        grad_pre = gpv[rows, :]
        total = jnp.zeros((CH, 128), F32)
        for t in range(tiles):
            cols = slice(t * TILE, (t + 1) * TILE)
            p = jnp.dot(grad_pre, wt[:, cols], preferred_element_type=F32)
            both = p * normed[rows, cols]
            gacc[:, cols] += both
            h = p * gain_ref[:, cols]
            gs[:, cols] = h
            weighted = both * gain_ref[:, cols]
            for i in range(TILE // 128):
                total = total + weighted[:, i * 128:(i + 1) * 128]
        center = jnp.sum(total, axis=1, keepdims=True) * (1.0 / feats)
        scale = inv[rows, 0:1]
        for t in range(tiles):
            cols = slice(t * TILE, (t + 1) * TILE)
            gin_ref[rows, cols] = (
                gbuf[rows, cols].astype(F32) + scale * (gs[:, cols] - normed[rows, cols] * center)
            ).astype(BF)

        @pl.when((s > 0) & (s != half))
        def _():
            down(gin_ref, gbuf, k, g_s, g_r).start()

        @pl.when(s > half)
        def _():
            term(k)
            down(tsend, tbuf, k, t_s, t_r).start()

        for g, (start, size) in enumerate(groups[:-1]):
            @pl.when(k == (start + size) // CH - 1)
            def _(g=g):
                late_send(g)
                own_rows(g)

        @pl.when(encoder & (k == 3))
        def _():
            sag.pair_step(last_pair - 2)
            sag.pair_step(last_pair - 1)

        for g, at in ((0, 5), (1, 6)):
            @pl.when(encoder & (k == at))
            def _(g=g):
                late_recv(g)
                late_pass(g).start()

        for up, at in ((0, 2), (1, 0)):
            @pl.when(decoder & (above == up) & (k == at))
            def _():
                sag.begin_other()

        for up, at, i in passing:
            @pl.when(decoder & (above == up) & (k == at))
            def _(i=i):
                sag.pair_step(i)

        return carry

    lax.fori_loop(0, n_ch, chunk, 0)

    late_send(len(groups) - 1)
    part = gacc[...]
    for q in range(nq):
        gnv[q] = part[0:8, q * 128:(q + 1) * 128] + part[8:16, q * 128:(q + 1) * 128]

    def gain_send(i, carry):
        q = lax.rem(q0 + i, nq)
        pltpu.make_async_remote_copy(
            src_ref=gnv.at[q], dst_ref=gng.at[q0], send_sem=tail_s.at[2], recv_sem=tail_r.at[2],
            device_id={"dp": q * 2 + c}, device_id_type=MESH).start()
        return carry

    lax.fori_loop(1, nq, gain_send, 0)
    gng[q0] = gnv[q0]
    store_gin = load(gin_ref, gin_hbm, 5)

    own_rows(len(groups) - 1)

    @pl.when(decoder)
    def _():
        for i in range(2, last_pair):
            @pl.when(i >= 2 + above)
            def _(i=i):
                sag.pair_step(i)

            if 3 <= i:
                late_recv(i - 3)
                late_pass(i - 3).start()
        for g in range(len(groups)):
            late_pass(g).wait_recv()

    @pl.when(encoder)
    def _():
        late_recv(2)
        late_pass(0).wait_recv()
        late_pass(1).wait_recv()

    most = toks - 2 * CH
    kk = nq * most
    parts = width // TILE
    gpt[:, 0:kk] = gpg[:, 0:most, :].reshape(kk, cols_z).T

    def product(t, carry):
        cols = cols_of(t)
        dwt[:, cols] = jnp.dot(gpt[:, 0:kk], sg[:, 0:most, cols].reshape(kk, TILE), preferred_element_type=F32)
        return carry

    lax.fori_loop(0, parts, product, 0, unroll=2)

    @pl.when(encoder)
    def _():
        late_recv(3)
        late_recv(4)

    gpt[:, kk:nq * toks] = gpg[:, most:toks, :].reshape(nq * 2 * CH, cols_z).T

    other = {"dp": q0 * 2 + 1 - c}
    per = TILE // (2 * rw)
    first_part = z // per

    def swap(t):
        spots = pl.ds(t * per, per)
        return pltpu.make_async_remote_copy(
            src_ref=dws.at[spots, 1 - c], dst_ref=dwp.at[spots], send_sem=swap_s.at[0], recv_sem=swap_r.at[t],
            device_id=other, device_id_type=MESH)

    turns = [parts // 2] + [v for i in range(parts // 2 - 1, 0, -1) for v in (i, parts - i)] + [0]

    def finish(i):
        t = lax.rem(first_part + i, parts)
        cols = cols_of(t)
        p = dwt[:, cols] + jnp.dot(
            gpt[:, kk:nq * toks], sg[:, most:toks, cols].reshape(nq * 2 * CH, TILE), preferred_element_type=F32)
        dws[pl.ds(t * per, per)] = p.T.astype(BF).reshape(per, 2, rw, cols_z)
        swap(t).start()

    for i in turns:
        finish(i)

    def deliver(i):
        t = lax.rem(first_part + i, parts)
        swap(t).wait_recv()
        for e in range(per):
            zz = t * per + e
            dwo[zz] = (dws[zz, c].astype(F32) + dwp[zz].astype(F32)).astype(BF)

            @pl.when(zz != z)
            def _(zz=zz):
                pltpu.make_async_remote_copy(
                    src_ref=dwo.at[zz], dst_ref=og.at[z], send_sem=tail_s.at[1], recv_sem=tail_r.at[1],
                    device_id=device(y, zz, c), device_id_type=MESH).start()

    for i in turns:
        deliver(i)
    store_own = load(dwo.at[z], og.at[z], 0)

    gain_all = pltpu.make_async_remote_copy(
        src_ref=gng.at[pl.ds(0, nq - 1)], dst_ref=gng.at[pl.ds(0, nq - 1)], send_sem=tail_s.at[2],
        recv_sem=tail_r.at[2], device_id=other, device_id_type=MESH)
    gain_all.wait()
    gnl[...] = jnp.sum(gng[...], axis=0)
    gain_copy = pltpu.make_async_remote_copy(
        src_ref=gnl, dst_ref=gnp, send_sem=tail_s.at[0], recv_sem=tail_r.at[0], device_id=other, device_id_type=MESH)
    gain_copy.start()

    near = sum(size for g, (_, size) in enumerate(groups) if g not in direct)
    both = toks - near

    @pl.when(encoder)
    def _():
        left(gpg.at[pl.ds(0, (near * (nz - 1) + both * (nq - 1)) // toks)], late_s.at[0], other)
        left(gpg.at[pl.ds(0, near * nz // toks)], pass_s.at[0], other)

    @pl.when(decoder)
    def _():
        left(gpg.at[pl.ds(0, nz - 1)], late_s.at[0], other)
        left(gpg.at[pl.ds(0, nz)], pass_s.at[0], other)

    @pl.when((s > 0) & (s != half))
    def _():
        left(gin_ref, g_s.at[0], other)

    @pl.when(decoder)
    def _():
        left(tsend, t_s.at[0], other)

    sag.sent()

    @pl.when(decoder)
    def _():
        wag.sent()
        relay.sent(False)

    @pl.when(encoder)
    def _():
        relay.sent(True)

    left(dwp, swap_s.at[0], other)
    store_gin.wait()
    gain_copy.wait()
    gains = jnp.sum(gnl[...] + gnp[...], axis=0, keepdims=True) * (1.0 / n_dp)
    gg_ref[...] = jnp.where(c == 0, gains[:, 0:rw], gains[:, rw:2 * rw])

    whole = pltpu.make_async_remote_copy(
        src_ref=dwo.at[pl.ds(0, nz - 1)], dst_ref=og.at[pl.ds(0, nz - 1)], send_sem=tail_s.at[1],
        recv_sem=tail_r.at[1], device_id=other, device_id_type=MESH)
    store_own.wait()
    whole.wait()


def publish_kernel(n_dp, gin_ref, blocks_ref, gain_ref, gin_out, dw_out, gain_out):
    gin_out[...] = gin_ref[...]
    nz, _, cols_z = blocks_ref.shape
    for zz in range(nz):
        dw_out[:, zz * cols_z:(zz + 1) * cols_z] = blocks_ref[zz].astype(F32) * (1.0 / n_dp)
    gain_out[...] = gain_ref[...]


def local(section_inputs, section_weights, memory_weights, norm_gains, memory, cotangent, lengths):
    n_sec, n_dp = lax.axis_size("section"), lax.axis_size("dp")
    toks, feats = section_inputs.shape[1:]
    rw = memory_weights.shape[1]
    nq = n_dp // 2
    nz = nq // 2
    n_ch = toks // CH
    vmem = pl.BlockSpec(memory_space=pltpu.VMEM)
    hbm = pl.BlockSpec(memory_space=pl.ANY)
    square = pltpu.VMEM((feats, feats), BF)
    wide = pltpu.VMEM((toks, feats), F32)
    narrow = pltpu.VMEM((toks, feats), BF)
    cols_z = feats // nz
    blocks = pltpu.VMEM((nz, rw, cols_z), BF)
    dma = pltpu.SemaphoreType.DMA
    gin, dw, gg = pl.pallas_call(
        functools.partial(relay_kernel, n_sec, n_dp),
        out_shape=(
            jax.ShapeDtypeStruct((toks, feats), BF),
            jax.ShapeDtypeStruct((nz, rw, cols_z), BF),
            jax.ShapeDtypeStruct((1, rw), F32),
        ),
        in_specs=[hbm, hbm, hbm, vmem, hbm, hbm, pl.BlockSpec(memory_space=pltpu.SMEM)],
        out_specs=(hbm, hbm, vmem),
        scratch_shapes=[
            narrow, narrow, narrow, narrow,
            square, square, square, square, narrow,
            pltpu.VMEM((nq, toks, feats // 2), BF),
            wide, wide, wide, wide,
            pltpu.VMEM((cols_z, feats // 2), F32),
            pltpu.VMEM((toks, 128), F32),
            narrow, narrow, narrow,
            narrow,
            pltpu.VMEM((CH, feats), F32),
            pltpu.VMEM((CH, feats), F32),
            pltpu.VMEM((CH, feats), F32),
            pltpu.VMEM((nq, toks, cols_z), BF),
            pltpu.VMEM((cols_z, nq * toks), BF),
            pltpu.VMEM((nz, 2, rw, cols_z), BF),
            blocks, blocks,
            pltpu.VMEM((nq, 8, 128), F32),
            pltpu.VMEM((nq, 8, 128), F32),
            pltpu.VMEM((8, 128), F32),
            pltpu.VMEM((8, 128), F32),
            dma((6,)),
            dma((1,)), dma((Gather.count(nz),)),
            dma((1,)), dma((Relay.count(nz),)),
            dma((1,)), dma((HalfGather.count(nz),)),
            dma((1,)), dma((n_ch,)), dma((1,)), dma((n_ch,)),
            dma((1,)), dma((5,)),
            dma((1,)), dma((5,)),
            dma((1,)), dma((feats // 2 // TILE,)),
            dma((3,)), dma((3,)),
        ],
        compiler_params=pltpu.CompilerParams(
            collective_id=0, has_side_effects=True, vmem_limit_bytes=60 * 1024 * 1024
        ),
    )(
        section_inputs[0], section_weights[0], memory_weights[0], norm_gains, memory, cotangent,
        lengths,
    )
    gin, dw, gg = pl.pallas_call(
        functools.partial(publish_kernel, n_dp),
        out_shape=(
            jax.ShapeDtypeStruct((toks, feats), BF),
            jax.ShapeDtypeStruct((rw, feats), F32),
            jax.ShapeDtypeStruct((1, rw), F32),
        ),
        in_specs=[vmem] * 3,
        out_specs=(vmem,) * 3,
    )(gin, dw, gg)
    return gin[None], dw[None], gg


def solution(mesh):
    return jax.shard_map(
        local,
        mesh=mesh,
        in_specs=(
            P("section", "dp", None),
            P("section", None, None),
            P("section", "dp", None),
            P("section", None),
            P("dp", None),
            P("dp", None),
            P("dp"),
        ),
        out_specs=(P("section", "dp", None), P("section", "dp", None), P("section", "dp")),
        check_vma=False,
    )
```

profile of v0, /device:TPU:1, one launch (start us, length us, event | category | flops | bytes accessed | tf_op | source)
XLA Modules:
  0.0 121.3 jit_solution(12315833801223612326)
XLA Ops:
  1.3 117.9 %shard_map.94 = (bf16[128,2048]{1,0:T(8,128)(2,1)}, bf16[8,64,256]{2,1,0:T(8,128)(2,1)}, f32[1,64]{1,0:T(1,128)}) custom-call(bf16[128,2048]{1,0:T(8,128)(2,1)} %bitcast.6, bf16[2048,2048]{1,0:T(8,128)(2,1)} %bitcast.5, bf16[64,2048]{1,0:T(8,128)(2,1)} %bitcast.7, f32[1,2048]{1,0:T(1,128)} %gain_ref.1, bf16[128,2048]{1,0:T(8,128)(2,1)} %mem_hbm.1, ...), custom_call_target="tpu_custom_call" | custom-call | tf_op jit(solution)/shard_map/pallas_call | solution.py:859
  119.2 2.2 %shard_map.95 = (bf16[128,2048]{1,0:T(8,128)(2,1)}, f32[64,2048]{1,0:T(8,128)}, f32[1,64]{1,0:T(1,128)}) custom-call(bf16[128,2048]{1,0:T(8,128)(2,1)} %get-tuple-element.9.gin_ref, bf16[8,64,256]{2,1,0:T(8,128)(2,1)} %get-tuple-element.10.blocks_ref, f32[1,64]{1,0:T(1,128)} %get-tuple-element.11.gain_ref), custom_call_target="tpu_custom_call" | custom-call | tf_op jit(solution)/shard_map/pallas_call | solution.py:905
where the time goes:
time: 122 us; the launch traced here: 121 us
  Pallas kernels  120 us (98%)
  between operations  1.29 us (1%)
    pallas_call x1, Pallas kernels, local(): pl.pallas_call(functools.partial(relay_kernel, n_sec, n_dp), out_shape=(j...  118 us

commit v1 on v0

--- a/solution.py
+++ b/solution.py
@@ -214,15 +214,14 @@
             self.ring(way, 1, 1).start()
         self.back(0, 0, 1).start()
 
-    def step(self, d):
+    def step(self, d, m):
         g = self.g
-        for m in (0, 1):
-            came = [args for args in g.backs(d) if args[2] == m]
-            self.await_quarters(len(came), 2 + 2 * (d - 1) + m)
-            for way, _, _ in came:
-                if d < g.far and (way, d + 1, m) in g.backs(d + 1):
-                    self.ring(way, d + 1, m).start()
-                self.back(way, d, m).start()
+        came = [args for args in g.backs(d) if args[2] == m]
+        self.await_quarters(len(came), 2 + 2 * (d - 1) + m)
+        for way, _, _ in came:
+            if d < g.far and (way, d + 1, m) in g.backs(d + 1):
+                self.ring(way, d + 1, m).start()
+            self.back(way, d, m).start()
 
     def sent(self, encoder):
         number = 2 + 2 * sum(len(self.g.backs(d)) for d in range(1, self.g.far + 1)) if encoder else 1
@@ -389,6 +388,14 @@
     def _():
         sag.cross(crossing).start()
         relay.begin()
+        relay.step(1, 0)
+        relay.begin_other()
+        for d in range(2, far + 1):
+            relay.step(d, 0)
+            relay.step(d - 1, 1)
+        relay.step(far, 1)
+        sag.begin()
+        sag.begin_other()
 
     load_w.wait()
 
@@ -403,14 +410,7 @@
         slope[:, cols] = sig * (1.0 + p * (1.0 - sig))
         return carry
 
-    lax.fori_loop(0, tiles // 2, preact_tile, 0)
-
-    @pl.when(encoder)
-    def _():
-        relay.begin_other()
-        relay.step(1)
-
-    lax.fori_loop(tiles // 2, tiles, preact_tile, 0)
+    lax.fori_loop(0, tiles, preact_tile, 0)
     load_mem.wait()
     load_cot.wait()
 
@@ -507,15 +507,8 @@
 
     @pl.when(encoder)
     def _():
-        relay.step(2)
-        turn_w(0, 4)
-        relay.step(3)
-        turn_w(1, 4)
-        relay.step(4)
-        sag.begin()
-        sag.begin_other()
-        turn_w(2, 4)
-        turn_w(3, 4)
+        for piece in range(4):
+            turn_w(piece, 4)
         for i in range(last_pair - 2):
             sag.pair_step(i)
 
@@ -652,36 +645,47 @@
             term(k)
             down(tsend, tbuf, k, t_s, t_r).start()
 
-        for g, (start, size) in enumerate(groups[:-1]):
-            @pl.when(k == (start + size) // CH - 1)
-            def _(g=g):
-                late_send(g)
-                own_rows(g)
-
-        @pl.when(encoder & (k == 3))
-        def _():
-            sag.pair_step(last_pair - 2)
-            sag.pair_step(last_pair - 1)
-
-        for g, at in ((0, 5), (1, 6)):
-            @pl.when(encoder & (k == at))
-            def _(g=g):
-                late_recv(g)
-                late_pass(g).start()
-
-        for up, at in ((0, 2), (1, 0)):
-            @pl.when(decoder & (above == up) & (k == at))
+        @pl.when(encoder)
+        def _():
+            for g, (start, size) in enumerate(groups[:-1]):
+                @pl.when(k == (start + size) // CH - 1)
+                def _(g=g):
+                    late_send(g)
+                    own_rows(g)
+
+            @pl.when(k == 3)
             def _():
-                sag.begin_other()
-
-        for up, at, i in passing:
-            @pl.when(decoder & (above == up) & (k == at))
-            def _(i=i):
-                sag.pair_step(i)
+                sag.pair_step(last_pair - 2)
+                sag.pair_step(last_pair - 1)
+
+            for g, at in ((0, 5), (1, 6)):
+                @pl.when(k == at)
+                def _(g=g):
+                    late_recv(g)
+                    late_pass(g).start()
+
+        for up in range(half):
+            @pl.when(above == up)
+            def _(up=up):
+                for at in {0: (2,), 1: (0,)}.get(up, ()):
+                    @pl.when(k == at)
+                    def _():
+                        sag.begin_other()
+
+                for at, i in [(at, i) for v, at, i in passing if v == up]:
+                    @pl.when(k == at)
+                    def _(i=i):
+                        sag.pair_step(i)
 
         return carry
 
     lax.fori_loop(0, n_ch, chunk, 0)
+
+    @pl.when(decoder)
+    def _():
+        for g in range(len(groups) - 1):
+            late_send(g)
+            own_rows(g)
 
     late_send(len(groups) - 1)
     part = gacc[...]

time: 122 us -> 122 us (level)
  no operation moved by 1% of the time
where the time goes in v1:
time: 122 us; the launch traced here: 121 us
  Pallas kernels  120 us (98%)
  between operations  1.29 us (1%)
    pallas_call x1, Pallas kernels, local(): pl.pallas_call(functools.partial(relay_kernel, n_sec, n_dp), out_shape=(j...  118 us

profile of v1, /device:TPU:1, one launch (start us, length us, event | category | flops | bytes accessed | tf_op | source)
XLA Modules:
  0.0 121.4 jit_solution(11168893288712843366)
XLA Ops:
  1.3 117.9 %shard_map.94 = (bf16[128,2048]{1,0:T(8,128)(2,1)}, bf16[8,64,256]{2,1,0:T(8,128)(2,1)}, f32[1,64]{1,0:T(1,128)}) custom-call(bf16[128,2048]{1,0:T(8,128)(2,1)} %bitcast.6, bf16[2048,2048]{1,0:T(8,128)(2,1)} %bitcast.5, bf16[64,2048]{1,0:T(8,128)(2,1)} %bitcast.7, f32[1,2048]{1,0:T(1,128)} %gain_ref.1, bf16[128,2048]{1,0:T(8,128)(2,1)} %mem_hbm.1, ...), custom_call_target="tpu_custom_call" | custom-call | tf_op jit(solution)/shard_map/pallas_call | solution.py:863
  119.2 2.2 %shard_map.95 = (bf16[128,2048]{1,0:T(8,128)(2,1)}, f32[64,2048]{1,0:T(8,128)}, f32[1,64]{1,0:T(1,128)}) custom-call(bf16[128,2048]{1,0:T(8,128)(2,1)} %get-tuple-element.9.gin_ref, bf16[8,64,256]{2,1,0:T(8,128)(2,1)} %get-tuple-element.10.blocks_ref, f32[1,64]{1,0:T(1,128)} %get-tuple-element.11.gain_ref), custom_call_target="tpu_custom_call" | custom-call | tf_op jit(solution)/shard_map/pallas_call | solution.py:909

commit v2 on v1

--- a/solution.py
+++ b/solution.py
@@ -610,6 +610,11 @@
         def _():
             down(gin_ref, gbuf, k, g_s, g_r).wait_recv()
 
+        @pl.when(encoder & (k == 6))
+        def _():
+            late_recv(1)
+            late_pass(1).start()
+
         @pl.when(s == half)
         def _():
             term(k)
@@ -658,11 +663,10 @@
                 sag.pair_step(last_pair - 2)
                 sag.pair_step(last_pair - 1)
 
-            for g, at in ((0, 5), (1, 6)):
-                @pl.when(k == at)
-                def _(g=g):
-                    late_recv(g)
-                    late_pass(g).start()
+            @pl.when(k == 5)
+            def _():
+                late_recv(0)
+                late_pass(0).start()
 
         for up in range(half):
             @pl.when(above == up)
@@ -712,9 +716,11 @@
             def _(i=i):
                 sag.pair_step(i)
 
-            if 3 <= i:
-                late_recv(i - 3)
-                late_pass(i - 3).start()
+            if 4 <= i:
+                late_recv(i - 4)
+                late_pass(i - 4).start()
+        late_recv(len(groups) - 1)
+        late_pass(len(groups) - 1).start()
         for g in range(len(groups)):
             late_pass(g).wait_recv()
 

time: 122 us -> 122 us (level)
  no operation moved by 1% of the time
where the time goes in v2:
time: 122 us
  Pallas kernels  121 us (99%)
  between operations  1.29 us (1%)
    pallas_call x1, Pallas kernels, local(): pl.pallas_call(functools.partial(relay_kernel, n_sec, n_dp), out_shape=(j...  118 us

profile of v2, /device:TPU:1, one launch (start us, length us, event | category | flops | bytes accessed | tf_op | source)
XLA Modules:
  0.0 121.8 jit_solution(1084930734066775976)
XLA Ops:
  1.3 118.4 %shard_map.94 = (bf16[128,2048]{1,0:T(8,128)(2,1)}, bf16[8,64,256]{2,1,0:T(8,128)(2,1)}, f32[1,64]{1,0:T(1,128)}) custom-call(bf16[128,2048]{1,0:T(8,128)(2,1)} %bitcast.6, bf16[2048,2048]{1,0:T(8,128)(2,1)} %bitcast.5, bf16[64,2048]{1,0:T(8,128)(2,1)} %bitcast.7, f32[1,2048]{1,0:T(1,128)} %gain_ref.1, bf16[128,2048]{1,0:T(8,128)(2,1)} %mem_hbm.1, ...), custom_call_target="tpu_custom_call" | custom-call | tf_op jit(solution)/shard_map/pallas_call | solution.py:869
  119.6 2.2 %shard_map.95 = (bf16[128,2048]{1,0:T(8,128)(2,1)}, f32[64,2048]{1,0:T(8,128)}, f32[1,64]{1,0:T(1,128)}) custom-call(bf16[128,2048]{1,0:T(8,128)(2,1)} %get-tuple-element.9.gin_ref, bf16[8,64,256]{2,1,0:T(8,128)(2,1)} %get-tuple-element.10.blocks_ref, f32[1,64]{1,0:T(1,128)} %get-tuple-element.11.gain_ref), custom_call_target="tpu_custom_call" | custom-call | tf_op jit(solution)/shard_map/pallas_call | solution.py:915
